TPU v7x, 256 devices: a whole 4x4x8 slice. The times are simulated.
256 devices in a mesh: pair: 32 (over y, z_lo, core), virt: 8 (over x, z_hi).
Axes of the slice: x: 4, y: 4, z: 8 (z_hi: 2, z_lo: 4; z = z_hi * 4 + z_lo), core: 2. Of those that a mesh axis runs over, the one named last changes fastest.
Arguments:
- amplitudes: bfloat16 [24576, 1024], P('pair'), may hold values from -24 to 24
- integrals: bfloat16 [1024, 8, 4096], P('pair', 'virt'), may hold values from -0.1875 to 0.1875
- pair_irrep: int32 [384], P('pair'), may hold values from 0 to 7
- cd_irrep: int32 [16], replicated, may hold values from 0 to 7, as said below
- mirror_tile: int32 [384], P('pair'), may hold values from 0 to 383, as said below
- pair_energy: float32 [24576], P('pair'), may hold values from -3 to -1
- virt_energy: float32 [8, 64], P('virt'), may hold values from 0.5 to 3
Outputs:
- update: bfloat16 [24576, 8, 4096], P('pair', 'virt')
Inputs may be any that keep to these rules, and one draw needn't show every extreme that they name: `mirror_tile`: the partner of a tile held on pair index p is held on pair index p + 32 / 2 modulo 32; the partner's partner is the tile itself. `cd_irrep`: when 16 >= 8 every label 0 to 7 is given to some block.
All inputs are finite; a program needn't handle non-finite values.
Results may differ from a plain program's by a relative error of at most 0.001.
Values may be sent and summed in bfloat16 or wider, within the bound.
No kernel may reach another device: no remote copies, remote signals or barrier semaphores. Data moves between devices by JAX's collectives and lax.ppermute only.
A program may use at most 128 MiB of HBM per device.

v0:
```python
import functools
import jax
import jax.numpy as jnp
import numpy as np
from jax import lax
from jax.experimental import pallas as pl
from jax.experimental.pallas import tpu as pltpu
from jax.sharding import PartitionSpec as P

BF = jnp.bfloat16
F32 = jnp.float32
I32 = jnp.int32
NT = (((1,), (1,)), ((), ()))
MIB = 1 << 20
SLOTS = 4
SPILL = 6
WIDE = 128


def place(y, z, core):
    return (y % 4) * 8 + z * 2 + core


def pairs_of(first, second):
    pairs = []
    for y in range(4):
        for z in range(4):
            for core, hop in enumerate((first, second)):
                if hop is not None:
                    pairs.append((place(y, z, core), place(*hop(y, z), core)))
    return pairs


def along_y(step):
    return lambda y, z: (y + step, z)


def along_z(flip):
    return lambda y, z: (y, z ^ flip)


def send(array, first, second):
    return lax.ppermute(array, "pair", pairs_of(first, second))


def swap_cores(array):
    return lax.ppermute(array, "pair", [(i, i ^ 1) for i in range(32)])


def order_table():
    table = np.zeros((32, 32), np.int32)
    for y in range(4):
        for z in range(4):
            for core in range(2):
                groups = []
                for chunk in range(4):
                    for side in (core, 1 - core):
                        one = {
                            1: ((y - 1, z), (y + 1, z)),
                            2: ((y, z ^ 1), (y, z ^ 2)),
                            3: ((y, z ^ 3), (y + 2, z)),
                            4: ((y - 1, z ^ 1), (y - 1, z ^ 2)),
                            5: ((y + 1, z ^ 1), (y + 1, z ^ 2)),
                            6: ((y - 1, z ^ 3), (y + 2, z ^ 1)),
                            7: ((y + 1, z ^ 3), (y + 2, z ^ 2)),
                        }
                        for piece in ((1, 2), (3, 4), (5, 6), (7,))[chunk]:
                            spot = one[piece][side]
                            groups += [place(*spot, 0), place(*spot, 1)]
                        if chunk == 3:
                            groups += [place(y, z, side), place(y + 2, z ^ 3, side)]
                table[place(y, z, core)] = groups
    return table


def params(mib):
    return pltpu.CompilerParams(vmem_limit_bytes=mib * MIB)


def cost(flops, bytes_accessed):
    return pl.CostEstimate(flops=0, bytes_accessed=0, transcendentals=0)


SMEM = pl.BlockSpec(memory_space=pltpu.SMEM)
VMEM = pl.BlockSpec(memory_space=pltpu.VMEM)
ANY = pl.BlockSpec(memory_space=pl.ANY)
LABELS = 16


def join_kernel(core_ref, own, other, after, out):
    core = core_ref[0]
    out[pl.ds(pl.multiple_of(core * 32, 32), 32), :] = own[...]
    out[pl.ds(pl.multiple_of(32 - core * 32, 32), 32), :] = other[...]


def join_cores(core, own, other, after):
    rows, columns = own.shape
    return pl.pallas_call(
        join_kernel,
        in_specs=[SMEM, VMEM, VMEM, ANY],
        out_specs=VMEM,
        out_shape=jax.ShapeDtypeStruct((2 * rows, columns), BF),
        compiler_params=params(8),
        cost_estimate=cost(0, 4 * rows * columns * 2),
    )(core, own, other, after)


def ranks_of(labels, blocks):
    ranks = []
    for b in range(blocks):
        rank = jnp.int32(0)
        for earlier in range(b):
            rank += (labels[earlier] == labels[b]).astype(I32)
        ranks.append(rank)
    return ranks


def spread(shape, axis, width, scalars):
    group = lax.broadcasted_iota(I32, shape, axis) // width
    out = jnp.full(shape, -1, I32)
    for i, scalar in enumerate(scalars):
        out = jnp.where(group == i, scalar, out)
    return out


def compact_kernel(first, slots, cd, irreps, amplitudes, out, masked):
    blocks = cd.shape[0]
    tiles = irreps.shape[0]
    rows, width = amplitudes.shape
    tile = rows // tiles
    block = width // blocks
    ranks = ranks_of(cd, blocks)
    label_row = spread((1, width), 1, block, [cd[b] for b in range(blocks)])
    for t in range(tiles):
        live = (label_row == irreps[t]).astype(F32).astype(BF)
        masked[t * tile : (t + 1) * tile, :] = amplitudes[t * tile : (t + 1) * tile, :] * live
    for half in range(slots * block // WIDE):
        column = lax.broadcasted_iota(I32, (block, WIDE), 1) + half * WIDE
        inner = lax.broadcasted_iota(I32, (block, WIDE), 0)
        choose = []
        for b in range(blocks):
            want = (ranks[b] - first) * block + inner
            choose.append((column == want).astype(F32).astype(BF))
        picked = jnp.dot(masked[...], jnp.concatenate(choose, 0), preferred_element_type=F32)
        out[:rows, half * WIDE : (half + 1) * WIDE] = picked.astype(BF)
    tags = spread((LABELS, slots * block), 0, 1, [irreps[t] for t in range(tiles)])
    out[rows:, :] = tags.astype(F32).astype(BF)


def compact(first, slots, cd, irreps, amplitudes):
    rows, width = amplitudes.shape
    block = width // cd.shape[0]
    return pl.pallas_call(
        functools.partial(compact_kernel, first, slots),
        in_specs=[SMEM, SMEM, VMEM],
        out_specs=VMEM,
        out_shape=jax.ShapeDtypeStruct((rows + LABELS, slots * block), BF),
        scratch_shapes=[pltpu.VMEM((rows, width), BF)],
        compiler_params=params(24),
        cost_estimate=cost(2 * rows * width * slots * block, rows * width * 2),
    )(cd, irreps, amplitudes)


def left_kernel(cd, irreps, mirror, order, amplitudes, sent, spill, out, rowed, rowed_spill):
    blocks = cd.shape[0]
    tiles = irreps.shape[0]
    rows, width = amplitudes.shape
    tile = rows // tiles
    block = width // blocks
    groups = order.shape[0]
    group = width // groups
    per = block // group
    ranks = ranks_of(cd, blocks)
    most = ranks[0]
    for rank in ranks[1:]:
        most = jnp.maximum(most, rank)
    sources = [lax.rem(mirror[t], tiles) for t in range(tiles)]
    for t in range(tiles):
        rows_t = pl.ds(pl.multiple_of(sources[t] * tile, tile), tile)
        rowed[t * tile : (t + 1) * tile, :] = sent[rows_t, :]

    @pl.when(most >= SLOTS)
    def _():
        for t in range(tiles):
            rows_t = pl.ds(pl.multiple_of(sources[t] * tile, tile), tile)
            rowed_spill[t * tile : (t + 1) * tile, :] = spill[rows_t, :]

    here = 2 * WIDE
    tags = sent[rows:, :].astype(F32)
    row = lax.broadcasted_iota(I32, tags.shape, 0)
    theirs = [jnp.where(row == sources[t], tags, 0.0).sum(0, keepdims=True) for t in range(tiles)]
    for part in range(width // here):
        mine = [order[part * (here // group) + i] for i in range(here // group)]
        lane = lax.broadcasted_iota(I32, (1, here), 1) % group
        origin = spread((1, here), 1, group, [owner * group for owner in mine]) + lane
        labels = spread((1, here), 1, group, [cd[owner // per] for owner in mine])
        rank_row = spread((1, here), 1, group, [rank_at(ranks, owner // per) for owner in mine])
        pick = (lax.broadcasted_iota(I32, (width, here), 0) == origin).astype(F32).astype(BF)
        moved = jnp.dot(amplitudes[...], pick, preferred_element_type=F32)
        slot = rank_row * block + origin % block
        pick = (lax.broadcasted_iota(I32, (SLOTS * block, here), 0) == slot).astype(F32).astype(BF)
        opened = jnp.dot(rowed[...], pick, preferred_element_type=F32)
        wanted = labels.astype(F32)
        for t in range(tiles):
            at = slice(t * tile, (t + 1) * tile)
            straight = jnp.where(labels == irreps[t], moved[at], 0.0).astype(BF)
            mirrored = jnp.where(wanted == theirs[t], opened[at], 0.0).astype(BF)
            for side in range(2):
                lanes = slice(side * WIDE, (side + 1) * WIDE)
                start = (4 * part + 2 * side) * WIDE
                out[at, start : start + WIDE] = straight[:, lanes]
                out[at, start + WIDE : start + 2 * WIDE] = mirrored[:, lanes]

        @pl.when(most >= SLOTS)
        def _():
            late = slot - SLOTS * block
            choose = (lax.broadcasted_iota(I32, (SPILL * block, here), 0) == late).astype(F32).astype(BF)
            rest = jnp.dot(rowed_spill[...], choose, preferred_element_type=F32)
            for t in range(tiles):
                at = slice(t * tile, (t + 1) * tile)
                mirrored = jnp.where(wanted == theirs[t], rest[at], 0.0).astype(BF)
                for side in range(2):
                    start = (4 * part + 2 * side + 1) * WIDE
                    out[at, start : start + WIDE] += mirrored[:, side * WIDE : (side + 1) * WIDE]


def rank_at(ranks, index):
    out = jnp.int32(0)
    for b, rank in enumerate(ranks):
        out = jnp.where(index == b, rank, out)
    return out


def left_sides(cd, irreps, mirror, order, amplitudes, sent, spill):
    rows, width = amplitudes.shape
    return pl.pallas_call(
        left_kernel,
        in_specs=[SMEM] * 4 + [VMEM] * 3,
        out_specs=VMEM,
        out_shape=jax.ShapeDtypeStruct((rows, 2 * width), BF),
        scratch_shapes=[pltpu.VMEM((rows, sent.shape[1]), BF), pltpu.VMEM((rows, spill.shape[1]), BF)],
        compiler_params=params(32),
        cost_estimate=cost(2 * rows * width * (width + sent.shape[1]), rows * width * 6),
    )(cd, irreps, mirror, order, amplitudes, sent, spill)


def turn_kernel(edge, count, *refs):
    pieces, out, held = refs[:count], refs[-2], refs[-1]
    for i in range(edge * edge // WIDE):
        columns = slice(i * WIDE, (i + 1) * WIDE)
        turned = jnp.concatenate([piece[:, columns] for piece in pieces], 0).T
        out[columns, :WIDE] = turned
        held[columns, :] = turned.astype(F32)
    for low in range(0, edge, 8):
        parts = []
        for b in range(0, edge, 8):
            rows = [held[(b + i) * edge + low : (b + i) * edge + low + 8, :] for i in range(8)]
            parts.append(jnp.swapaxes(jnp.stack(rows, 0), 0, 1))
        whole = jnp.concatenate(parts, 1)
        out[low * edge : (low + 8) * edge, WIDE:] = whole.reshape(8 * edge, WIDE).astype(BF)


def turn(edge, pieces, after=()):
    columns = edge * edge
    return pl.pallas_call(
        functools.partial(turn_kernel, edge, len(pieces)),
        in_specs=[VMEM] * len(pieces) + [ANY] * len(after),
        out_specs=VMEM,
        out_shape=jax.ShapeDtypeStruct((columns, 2 * WIDE), BF),
        scratch_shapes=[pltpu.VMEM((columns, WIDE), F32)],
        compiler_params=params(12),
        cost_estimate=cost(columns * WIDE * 2, columns * WIDE * 6),
    )(*pieces, *after)


def ladder_kernel(count, last, *refs):
    left = refs[0]
    sides = refs[1 : 1 + count]
    rest = refs[1 + count :]
    rows = left.shape[0]
    if last:
        held, row_energy, column_energy, out, spread_energy = rest

        @pl.when(pl.program_id(0) == 0)
        def _():
            for i in range(rows // WIDE):
                at = slice(i * WIDE, (i + 1) * WIDE)
                spread_energy[at, :] = jnp.broadcast_to(row_energy[:, at], (WIDE, WIDE)).T
    else:
        (out,) = rest
    narrow = 2 * WIDE
    for low in range(0, out.shape[1], narrow):
        right = jnp.concatenate([s[low : low + narrow, :] for s in sides], 1)
        total = lax.dot_general(left[...], right, NT, preferred_element_type=F32)
        if not last:
            out[:, low : low + narrow] = total
            continue
        for i in range(0, narrow, WIDE):
            at = slice(low + i, low + i + WIDE)
            denominator = column_energy[:, at] - spread_energy[...]
            out[:, at] = ((total[:, i : i + WIDE] + held[:, at]) / denominator).astype(BF)


def ladder(which, left, sides, held=None, row_energy=None, column_energy=None):
    last = held is not None
    rows = left.shape[0]
    columns = sides[0].shape[0]
    wide = 1024
    depth = len(sides) * 2 * WIDE
    right = pl.BlockSpec((wide, 2 * WIDE), lambda g: (g, 0))
    block = pl.BlockSpec((rows, wide), lambda g: (0, g))
    in_specs = [pl.BlockSpec((rows, depth), lambda g: (0, which))] + [right] * len(sides)
    args = [left, *sides]
    scratch = []
    if last:
        in_specs += [block, pl.BlockSpec((1, rows), lambda g: (0, 0)), pl.BlockSpec((1, wide), lambda g: (0, g))]
        args += [held, row_energy, column_energy]
        scratch = [pltpu.VMEM((rows, WIDE), F32)]
    return pl.pallas_call(
        functools.partial(ladder_kernel, len(sides), last),
        grid=(columns // wide,),
        in_specs=in_specs,
        out_specs=block,
        out_shape=jax.ShapeDtypeStruct((rows, columns), BF if last else F32),
        scratch_shapes=scratch,
        compiler_params=params(32),
        cost_estimate=cost(2 * rows * columns * depth, rows * columns * 6),
    )(*args)


def body(amplitudes, integrals, pair_irrep, cd_irrep, mirror_tile, pair_energy, virt_energy):
    rows = amplitudes.shape[0]
    edge = virt_energy.shape[1]
    columns = edge * edge
    me = lax.axis_index("pair")
    core = (me % 2).astype(I32)
    own = integrals.reshape(integrals.shape[0], columns)

    packed = compact(0, SLOTS, cd_irrep, pair_irrep, amplitudes)
    sent = send(packed, along_y(2), along_y(2))
    same = (cd_irrep[:, None] == cd_irrep[None, :]).astype(I32).sum(1)

    def more():
        return send(compact(SLOTS, SPILL, cd_irrep, pair_irrep, amplitudes), along_y(2), along_y(2))

    def none():
        return jnp.zeros((rows + LABELS, SPILL * edge), BF)

    spill = lax.cond(same.max() > SLOTS, more, none)

    block = join_cores(core.reshape(1), own, swap_cores(own), packed)
    p1 = send(block, along_y(1), along_y(-1))
    p2 = send(block, along_z(1), along_z(2))
    p3 = send(block, along_z(3), along_y(2))
    p4 = send(p2, along_y(1), along_y(1))
    p5 = send(p2, along_y(-1), along_y(-1))
    p6 = send(p3, along_y(1), along_z(1))
    p7 = send(p3, along_y(-1), along_z(2))
    half = lax.dynamic_slice(p3, (core * 32, jnp.int32(0)), (32, columns))
    p8 = send(half, along_y(2), along_z(3))

    order = jnp.asarray(order_table())[me]
    left = left_sides(cd_irrep, pair_irrep, mirror_tile, order, amplitudes, sent, spill)

    sides = []
    for pieces, after in (((p1, p2), (sent, spill)), ((p3, p4), (left,)), ((p5, p6), ()), ((p7, own, p8), ())):
        mine = turn(edge, pieces, after)
        sides += [mine, swap_cores(mine)]

    column_energy = (virt_energy[0][:, None] + virt_energy[0][None, :]).reshape(1, columns)
    row_energy = pair_energy.reshape(1, rows)
    held = ladder(0, left, sides[:4])
    out = ladder(1, left, sides[4:], held, row_energy, column_energy)
    return out.reshape(rows, 1, columns)


def solution(mesh):
    placed = (
        P("pair", None),
        P("pair", "virt", None),
        P("pair"),
        P(),
        P("pair"),
        P("pair"),
        P("virt", None),
    )
    return jax.shard_map(
        body, mesh=mesh, in_specs=placed, out_specs=P("pair", "virt", None), check_vma=False
    )
```

profile of v0, /device:TPU:1, one launch (start us, length us, event | category | flops | bytes accessed | tf_op | source)
XLA Modules:
  0.0 85.6 jit_solution(5131887465737214758)
XLA Ops:
  0.0 0.0 copy-start.6
  0.0 3.3 %collective-permute-start.2 = (bf16[32,4096]{1,0:T(8,128)(2,1)}, bf16[32,4096]{1,0:T(8,128)(2,1)S(1)}, u32[]{:S(2)}, u32[]{:S(2)}) collective-permute-start(bf16[32,4096]{1,0:T(8,128)(2,1)} %bitcast.6), channel_id=1, source_target_pairs={{0,8},{8,0},{16,24},{24,16},{32,40},{40,32},{48,56},{56,48},{64,72... | collective-permute-start | bytes 786440 | tf_op jit(solution)/shard_map/ppermute | solution.py:47
  3.3 2.4 %shard_map.82.after = bf16[784,256]{1,0:T(8,128)(2,1)S(1)} custom-call(s32[16]{0:T(128)} %cd.3, s32[12]{0:T(128)} %irreps.3, bf16[768,1024]{1,0:T(8,128)(2,1)} %amplitudes.3), custom_call_target="tpu_custom_call" | custom-call | tf_op jit(solution)/shard_map/pallas_call | solution.py:153
  5.7 0.0 collective-permute-done.2.other
  5.7 0.0 copy-done
  5.8 0.0 copy-start.4
  5.8 1.4 %collective-permute-start.3 = (bf16[64,4096]{1,0:T(8,128)(2,1)S(1)}, bf16[64,4096]{1,0:T(8,128)(2,1)}, u32[]{:S(2)}, u32[]{:S(2)}) collective-permute-start(bf16[64,4096]{1,0:T(8,128)(2,1)S(1)} %shard_map.84), channel_id=1, source_target_pairs={{0,16},{8,40},{16,0},{24,56},{32,48},{40,8},{48,32},{56,24},{64,80... | collective-permute-start | bytes 1572872 | tf_op jit(solution)/shard_map/ppermute | solution.py:43
  7.2 2.9 %collective-permute-start.5 = (bf16[64,4096]{1,0:T(8,128)(2,1)S(1)}, bf16[64,4096]{1,0:T(8,128)(2,1)}, u32[]{:S(2)}, u32[]{:S(2)}) collective-permute-start(bf16[64,4096]{1,0:T(8,128)(2,1)S(1)} %shard_map.84), channel_id=1, source_target_pairs={{0,48},{8,136},{16,32},{24,152},{32,16},{40,168},{48,0},{56,184},{... | collective-permute-start | bytes 1572872 | tf_op jit(solution)/shard_map/ppermute | solution.py:43
  10.1 0.1 collective-permute-start.1
  10.1 2.7 %collective-permute-start.11 = (bf16[64,4096]{1,0:T(8,128)(2,1)S(1)}, bf16[64,4096]{1,0:T(8,128)(2,1)S(1)}, u32[]{:S(2)}, u32[]{:S(2)}) collective-permute-start(bf16[64,4096]{1,0:T(8,128)(2,1)S(1)} %shard_map.84), channel_id=1, source_target_pairs={{0,64},{8,200},{16,80},{24,216},{32,96},{40,232},{48,112},{56,248}... | collective-permute-start | bytes 1572872 | tf_op jit(solution)/shard_map/ppermute | solution.py:43
  12.9 0.2 convert_reduce_fusion
  13.1 0.6 reduce_max.9
  14.4 0.9 %conditional.1 = (bf16[784,384]{1,0:T(8,128)(2,1)}) conditional(s32[]{:T(128)} %convert_element_type.7, () %tuple.11, (s32[16]{0:T(128)S(1)}, s32[12]{0:T(128)S(1)}, bf16[768,1024]{1,0:T(8,128)(2,1)S(1)}) %tuple.17), branch_computations={%region_2.3_spmd, %region_3.4_spmd} | conditional | bytes 2408496 | solution.py:349
  14.4 0.9 %broadcast.9 = bf16[784,384]{1,0:T(8,128)(2,1)} broadcast(bf16[]{:T(256)} %constant.10.clone), dimensions={} | broadcast | bytes 602114 | tf_op jit(solution)/shard_map/broadcast.1
  15.3 16.2 %collective-permute-done.3.refs_1_ = bf16[64,4096]{1,0:T(8,128)(2,1)} collective-permute-done((bf16[64,4096]{1,0:T(8,128)(2,1)S(1)}, bf16[64,4096]{1,0:T(8,128)(2,1)}, u32[]{:S(2)}, u32[]{:S(2)}) %collective-permute-start.3) | collective-permute-done | bytes 524320 | tf_op jit(solution)/shard_map/ppermute | solution.py:43
  31.5 0.0 collective-permute-start.13
  31.5 2.7 %collective-permute-start.4 = (bf16[64,4096]{1,0:T(8,128)(2,1)}, bf16[64,4096]{1,0:T(8,128)(2,1)}, u32[]{:S(2)}, u32[]{:S(2)}) collective-permute-start(bf16[64,4096]{1,0:T(8,128)(2,1)} %collective-permute-done.3.refs_1_), channel_id=1, source_target_pairs={{0,192},{8,200},{16,208},{24,216},{32,224},{40,232},{48,240},{56,2... | collective-permute-start | bytes 1572872 | tf_op jit(solution)/shard_map/ppermute | solution.py:43
  34.2 0.0 collective-permute-done.5.refs_0_
  34.2 0.0 collective-permute-start.8
  34.2 0.0 collective-permute-done.1.sent.refs_2_
  34.2 2.7 %collective-permute-start.6 = (bf16[64,4096]{1,0:T(8,128)(2,1)}, bf16[64,4096]{1,0:T(8,128)(2,1)}, u32[]{:S(2)}, u32[]{:S(2)}) collective-permute-start(bf16[64,4096]{1,0:T(8,128)(2,1)} %collective-permute-done.5.refs_0_), channel_id=1, source_target_pairs={{0,64},{8,24},{16,80},{24,8},{32,96},{40,56},{48,112},{56,40},{64,... | collective-permute-start | bytes 1572872 | tf_op jit(solution)/shard_map/ppermute | solution.py:43
  36.9 1.7 %constant_dynamic-slice_fusion = bf16[32,4096]{1,0:T(8,128)(2,1)} fusion(bf16[64,4096]{1,0:T(8,128)(2,1)} %collective-permute-done.5.refs_0_, s32[]{:T(128)S(6)} %select_n.15), kind=kLoop, calls=%fused_computation.3 | loop fusion | bytes 524292 | tf_op jit(solution)/shard_map/dynamic_slice | solution.py:359
  38.6 1.9 %collective-permute-done.11.refs_0_ = bf16[64,4096]{1,0:T(8,128)(2,1)S(1)} collective-permute-done((bf16[64,4096]{1,0:T(8,128)(2,1)S(1)}, bf16[64,4096]{1,0:T(8,128)(2,1)S(1)}, u32[]{:S(2)}, u32[]{:S(2)}) %collective-permute-start.11) | collective-permute-done | bytes 524320 | tf_op jit(solution)/shard_map/ppermute | solution.py:43
  40.5 0.8 copy-done.2
  41.3 0.1 collective-permute-start.9
  41.3 0.7 dynamic-slice_bitcast_fusion.order
  42.0 4.8 %shard_map.83.refs_2_.refs_0_ = bf16[768,2048]{1,0:T(8,128)(2,1)S(1)} custom-call(s32[16]{0:T(128)S(1)} %copy-done.6, s32[12]{0:T(128)} %irreps.3, s32[12]{0:T(128)S(1)} %copy-done.4, s32[32]{0:T(128)S(1)} %dynamic-slice_bitcast_fusion.order, bf16[768,1024]{1,0:T(8,128)(2,1)} %amplitudes.3, bf16[784,256]{1,0:T(8,128)(2,1)S(1)} %collective-permute-done.1.sent.refs_2_, ...), custom_call_target="tpu_custom_call" | custom-call | tf_op jit(solution)/shard_map/pallas_call | solution.py:236
  46.9 3.1 %shard_map.87.refs_1_ = bf16[4096,256]{1,0:T(8,128)(2,1)} custom-call(bf16[64,4096]{1,0:T(8,128)(2,1)S(1)} %copy-done.3, bf16[64,4096]{1,0:T(8,128)(2,1)} %collective-permute-done.3.refs_1_, bf16[784,256]{1,0:T(8,128)(2,1)S(1)} %collective-permute-done.1.sent.refs_2_, bf16[784,384]{1,0:T(8,128)(2,1)} %get-tuple-element.17.spill.refs_3_), custom_call_target="tpu_custom_call" | custom-call | tf_op jit(solution)/shard_map/pallas_call | solution.py:265
  50.0 0.0 collective-permute-done.13.refs_1_
  50.0 0.0 collective-permute-start.12
  50.0 3.3 %shard_map.88.refs_3_ = bf16[4096,256]{1,0:T(8,128)(2,1)} custom-call(bf16[64,4096]{1,0:T(8,128)(2,1)} %collective-permute-done.5.refs_0_, bf16[64,4096]{1,0:T(8,128)(2,1)} %collective-permute-done.13.refs_1_, bf16[768,2048]{1,0:T(8,128)(2,1)S(1)} %shard_map.83.refs_2_.refs_0_), custom_call_target="tpu_custom_call" | custom-call | tf_op jit(solution)/shard_map/pallas_call | solution.py:265
  53.3 0.0 collective-permute-done.9.refs_2_
  53.3 0.5 collective-permute-start.14
  53.7 0.0 collective-permute-done.8.refs_0_
  53.7 3.2 %shard_map.86.refs_3_ = bf16[4096,256]{1,0:T(8,128)(2,1)} custom-call(bf16[64,4096]{1,0:T(8,128)(2,1)} %collective-permute-done.8.refs_0_, bf16[32,4096]{1,0:T(8,128)(2,1)S(1)} %bitcast.8, bf16[32,4096]{1,0:T(8,128)(2,1)} %collective-permute-done.9.refs_2_), custom_call_target="tpu_custom_call" | custom-call | tf_op jit(solution)/shard_map/pallas_call | solution.py:265
  56.9 0.0 collective-permute-start.10
  57.0 0.0 collective-permute-done.4.refs_0_
  57.0 0.0 collective-permute-done.6.refs_1_
  57.0 3.3 %shard_map.85.refs_1_ = bf16[4096,256]{1,0:T(8,128)(2,1)} custom-call(bf16[64,4096]{1,0:T(8,128)(2,1)} %collective-permute-done.4.refs_0_, bf16[64,4096]{1,0:T(8,128)(2,1)} %collective-permute-done.6.refs_1_), custom_call_target="tpu_custom_call" | custom-call | tf_op jit(solution)/shard_map/pallas_call | solution.py:265
  60.3 0.5 collective-permute-start.7
  60.7 0.1 broadcast_add_fusion
  60.8 0.1 add.42.refs_7_
  60.9 0.0 collective-permute-done.12.refs_2_
  60.9 0.0 collective-permute-done.14.refs_4_
  60.9 11.5 %shard_map.89.refs_5_ = f32[768,4096]{1,0:T(8,128)} custom-call(bf16[768,2048]{1,0:T(8,128)(2,1)S(1)} %shard_map.83.refs_2_.refs_0_, bf16[4096,256]{1,0:T(8,128)(2,1)} %shard_map.87.refs_1_, bf16[4096,256]{1,0:T(8,128)(2,1)} %collective-permute-done.12.refs_2_, bf16[4096,256]{1,0:T(8,128)(2,1)} %shard_map.88.refs_3_, ...), custom_call_target="tpu_custom_call" | custom-call | tf_op jit(solution)/shard_map/pallas_call | solution.py:319
  72.4 0.0 collective-permute-done.10.refs_4_
  72.4 0.0 collective-permute-done.7.refs_2_
  72.4 13.2 %shard_map.90 = bf16[768,4096]{1,0:T(8,128)(2,1)} custom-call(bf16[768,2048]{1,0:T(8,128)(2,1)S(1)} %shard_map.83.refs_2_.refs_0_, bf16[4096,256]{1,0:T(8,128)(2,1)} %shard_map.85.refs_1_, bf16[4096,256]{1,0:T(8,128)(2,1)} %collective-permute-done.7.refs_2_, bf16[4096,256]{1,0:T(8,128)(2,1)} %shard_map.86.refs_3_, ...), custom_call_target="tpu_custom_call" | custom-call | tf_op jit(solution)/shard_map/pallas_call | solution.py:319
  (18 shorter events, 0.1 us)
Async XLA Ops:
  0.0 5.7 %copy-start = (bf16[32,1,4096]{2,0,1:T(8,128)(2,1)S(1)}, bf16[32,1,4096]{2,0,1:T(8,128)(2,1)}, u32[]{:S(2)}) copy-start(bf16[32,1,4096]{2,0,1:T(8,128)(2,1)} %param.11) | copy-start | bytes 786436
  0.0 14.4 %copy-start.5 = (bf16[768,1024]{1,0:T(8,128)(2,1)S(1)}, bf16[768,1024]{1,0:T(8,128)(2,1)}, u32[]{:S(2)}) copy-start(bf16[768,1024]{1,0:T(8,128)(2,1)} %amplitudes.3) | copy-start | bytes 4718596
  0.0 14.4 %copy-start.7 = (s32[12]{0:T(128)S(1)}, s32[12]{0:T(128)}, u32[]{:S(2)}) copy-start(s32[12]{0:T(128)} %irreps.3) | copy-start | bytes 148
  0.0 12.9 %copy-start.6 = (s32[16]{0:T(128)S(1)}, s32[16]{0:T(128)}, u32[]{:S(2)}) copy-start(s32[16]{0:T(128)} %cd.3) | copy-start | bytes 196
  0.0 5.7 %collective-permute-start.2 = (bf16[32,4096]{1,0:T(8,128)(2,1)}, bf16[32,4096]{1,0:T(8,128)(2,1)S(1)}, u32[]{:S(2)}, u32[]{:S(2)}) collective-permute-start(bf16[32,4096]{1,0:T(8,128)(2,1)} %bitcast.6), channel_id=1, source_target_pairs={{0,8},{8,0},{16,24},{24,16},{32,40},{40,32},{48,56},{56,48},{64,72... | collective-permute-start | bytes 786440 | tf_op jit(solution)/shard_map/ppermute | solution.py:47
  5.8 36.3 %copy-start.4 = (s32[12]{0:T(128)S(1)}, s32[12]{0:T(128)}, u32[]{:S(2)}) copy-start(s32[12]{0:T(128)} %mirror.1) | copy-start | bytes 148
  5.8 25.7 %collective-permute-start.3 = (bf16[64,4096]{1,0:T(8,128)(2,1)S(1)}, bf16[64,4096]{1,0:T(8,128)(2,1)}, u32[]{:S(2)}, u32[]{:S(2)}) collective-permute-start(bf16[64,4096]{1,0:T(8,128)(2,1)S(1)} %shard_map.84), channel_id=1, source_target_pairs={{0,16},{8,40},{16,0},{24,56},{32,48},{40,8},{48,32},{56,24},{64,80... | collective-permute-start | bytes 1572872 | tf_op jit(solution)/shard_map/ppermute | solution.py:43
  7.2 27.0 %collective-permute-start.5 = (bf16[64,4096]{1,0:T(8,128)(2,1)S(1)}, bf16[64,4096]{1,0:T(8,128)(2,1)}, u32[]{:S(2)}, u32[]{:S(2)}) collective-permute-start(bf16[64,4096]{1,0:T(8,128)(2,1)S(1)} %shard_map.84), channel_id=1, source_target_pairs={{0,48},{8,136},{16,32},{24,152},{32,16},{40,168},{48,0},{56,184},{... | collective-permute-start | bytes 1572872 | tf_op jit(solution)/shard_map/ppermute | solution.py:43
  10.1 24.1 %collective-permute-start.1 = (bf16[784,256]{1,0:T(8,128)(2,1)S(1)}, bf16[784,256]{1,0:T(8,128)(2,1)S(1)}, u32[]{:S(2)}, u32[]{:S(2)}) collective-permute-start(bf16[784,256]{1,0:T(8,128)(2,1)S(1)} %shard_map.82.after), channel_id=1, source_target_pairs={{0,128},{8,136},{16,144},{24,152},{32,160},{40,168},{48,176},{56,1... | collective-permute-start | bytes 1204232 | tf_op jit(solution)/shard_map/ppermute | solution.py:43
  10.1 30.3 %collective-permute-start.11 = (bf16[64,4096]{1,0:T(8,128)(2,1)S(1)}, bf16[64,4096]{1,0:T(8,128)(2,1)S(1)}, u32[]{:S(2)}, u32[]{:S(2)}) collective-permute-start(bf16[64,4096]{1,0:T(8,128)(2,1)S(1)} %shard_map.84), channel_id=1, source_target_pairs={{0,64},{8,200},{16,80},{24,216},{32,96},{40,232},{48,112},{56,248}... | collective-permute-start | bytes 1572872 | tf_op jit(solution)/shard_map/ppermute | solution.py:43
  31.5 18.4 %collective-permute-start.13 = (bf16[64,4096]{1,0:T(8,128)(2,1)}, bf16[64,4096]{1,0:T(8,128)(2,1)}, u32[]{:S(2)}, u32[]{:S(2)}) collective-permute-start(bf16[64,4096]{1,0:T(8,128)(2,1)} %collective-permute-done.3.refs_1_), channel_id=1, source_target_pairs={{0,64},{8,72},{16,80},{24,88},{32,96},{40,104},{48,112},{56,120},{... | collective-permute-start | bytes 1572872 | tf_op jit(solution)/shard_map/ppermute | solution.py:43
  31.5 25.4 %collective-permute-start.4 = (bf16[64,4096]{1,0:T(8,128)(2,1)}, bf16[64,4096]{1,0:T(8,128)(2,1)}, u32[]{:S(2)}, u32[]{:S(2)}) collective-permute-start(bf16[64,4096]{1,0:T(8,128)(2,1)} %collective-permute-done.3.refs_1_), channel_id=1, source_target_pairs={{0,192},{8,200},{16,208},{24,216},{32,224},{40,232},{48,240},{56,2... | collective-permute-start | bytes 1572872 | tf_op jit(solution)/shard_map/ppermute | solution.py:43
  34.2 19.5 %collective-permute-start.8 = (bf16[64,4096]{1,0:T(8,128)(2,1)}, bf16[64,4096]{1,0:T(8,128)(2,1)}, u32[]{:S(2)}, u32[]{:S(2)}) collective-permute-start(bf16[64,4096]{1,0:T(8,128)(2,1)} %collective-permute-done.5.refs_0_), channel_id=1, source_target_pairs={{0,192},{8,40},{16,208},{24,56},{32,224},{40,8},{48,240},{56,24},{... | collective-permute-start | bytes 1572872 | tf_op jit(solution)/shard_map/ppermute | solution.py:43
  34.2 22.8 %collective-permute-start.6 = (bf16[64,4096]{1,0:T(8,128)(2,1)}, bf16[64,4096]{1,0:T(8,128)(2,1)}, u32[]{:S(2)}, u32[]{:S(2)}) collective-permute-start(bf16[64,4096]{1,0:T(8,128)(2,1)} %collective-permute-done.5.refs_0_), channel_id=1, source_target_pairs={{0,64},{8,24},{16,80},{24,8},{32,96},{40,56},{48,112},{56,40},{64,... | collective-permute-start | bytes 1572872 | tf_op jit(solution)/shard_map/ppermute | solution.py:43
  40.5 0.8 copy-start.2
  41.3 12.0 %collective-permute-start.9 = (bf16[32,4096]{1,0:T(8,128)(2,1)}, bf16[32,4096]{1,0:T(8,128)(2,1)}, u32[]{:S(2)}, u32[]{:S(2)}) collective-permute-start(bf16[32,4096]{1,0:T(8,128)(2,1)} %constant_dynamic-slice_fusion), channel_id=1, source_target_pairs={{0,128},{8,56},{16,144},{24,40},{32,160},{40,24},{48,176},{56,8},{... | collective-permute-start | bytes 786440 | tf_op jit(solution)/shard_map/ppermute | solution.py:43
  42.0 4.8 %copy-start.3 = (bf16[64,4096]{1,0:T(8,128)(2,1)S(1)}, bf16[64,4096]{1,0:T(8,128)(2,1)}, u32[]{:S(2)}) copy-start(bf16[64,4096]{1,0:T(8,128)(2,1)} %copy-done.2) | copy-start | bytes 1572868
  50.0 3.8 %copy-start.1 = (bf16[32,1,4096]{2,0,1:T(8,128)(2,1)S(1)}, bf16[32,1,4096]{2,0,1:T(8,128)(2,1)}, u32[]{:S(2)}) copy-start(bf16[32,1,4096]{2,0,1:T(8,128)(2,1)} %param.11) | copy-start | bytes 786436
  50.0 10.9 %collective-permute-start.12 = (bf16[4096,256]{1,0:T(8,128)(2,1)}, bf16[4096,256]{1,0:T(8,128)(2,1)}, u32[]{:S(2)}, u32[]{:S(2)}) collective-permute-start(bf16[4096,256]{1,0:T(8,128)(2,1)} %shard_map.87.refs_1_), channel_id=1, source_target_pairs={{0,8},{8,0},{16,24},{24,16},{32,40},{40,32},{48,56},{56,48},{64,72... | collective-permute-start | bytes 6291464 | tf_op jit(solution)/shard_map/ppermute | solution.py:47
  53.3 7.7 %collective-permute-start.14 = (bf16[4096,256]{1,0:T(8,128)(2,1)}, bf16[4096,256]{1,0:T(8,128)(2,1)}, u32[]{:S(2)}, u32[]{:S(2)}) collective-permute-start(bf16[4096,256]{1,0:T(8,128)(2,1)} %shard_map.88.refs_3_), channel_id=1, source_target_pairs={{0,8},{8,0},{16,24},{24,16},{32,40},{40,32},{48,56},{56,48},{64,72... | collective-permute-start | bytes 6291464 | tf_op jit(solution)/shard_map/ppermute | solution.py:47
  56.9 3.8 %copy-start.9 = (f32[1,64]{1,0:T(1,128)S(1)}, f32[1,64]{1,0:T(1,128)}, u32[]{:S(2)}) copy-start(f32[1,64]{1,0:T(1,128)} %param.16) | copy-start | bytes 772
  56.9 4.0 %copy-start.8 = (f32[768]{0:T(1024)S(1)}, f32[768]{0:T(1024)}, u32[]{:S(2)}) copy-start(f32[768]{0:T(1024)} %param.15) | copy-start | bytes 9220
  56.9 15.5 %collective-permute-start.10 = (bf16[4096,256]{1,0:T(8,128)(2,1)}, bf16[4096,256]{1,0:T(8,128)(2,1)}, u32[]{:S(2)}, u32[]{:S(2)}) collective-permute-start(bf16[4096,256]{1,0:T(8,128)(2,1)} %shard_map.86.refs_3_), channel_id=1, source_target_pairs={{0,8},{8,0},{16,24},{24,16},{32,40},{40,32},{48,56},{56,48},{64,72... | collective-permute-start | bytes 6291464 | tf_op jit(solution)/shard_map/ppermute | solution.py:47
  60.3 12.2 %collective-permute-start.7 = (bf16[4096,256]{1,0:T(8,128)(2,1)}, bf16[4096,256]{1,0:T(8,128)(2,1)}, u32[]{:S(2)}, u32[]{:S(2)}) collective-permute-start(bf16[4096,256]{1,0:T(8,128)(2,1)} %shard_map.85.refs_1_), channel_id=1, source_target_pairs={{0,8},{8,0},{16,24},{24,16},{32,40},{40,32},{48,56},{56,48},{64,72... | collective-permute-start | bytes 6291464 | tf_op jit(solution)/shard_map/ppermute | solution.py:47
where the time goes:
time: 86 us; the launch traced here: 85.6 us
  Pallas kernels  44.8 us (52%)
  waiting for transfers between devices  18.2 us (21%)
  starting transfers between devices  16.8 us (20%)
  local copies, waits for them, and re-layouts  4.19 us (5%)
  other arithmetic  0.89 us (1%)
    pallas_call x2, Pallas kernels, ladder(): pl.pallas_call(functools.partial(ladder_kernel, len(sides), last), grid=(...  24.7 us
    ppermute x9, waiting for transfers between devices, send(): return lax.ppermute(array, 'pair', pairs_of(first, second))  18.1 us
    pallas_call x4, Pallas kernels, turn(): pl.pallas_call(functools.partial(turn_kernel, edge, len(pieces)), in_spec...  12.8 us
    ppermute x9, starting transfers between devices, send(): return lax.ppermute(array, 'pair', pairs_of(first, second))  12.5 us
    pallas_call x1, Pallas kernels, left_sides(): pl.pallas_call(left_kernel, in_specs=[SMEM] * 4 + [VMEM] * 3, out_specs=V...  4.83 us
    ppermute x5, starting transfers between devices, swap_cores(): return lax.ppermute(array, 'pair', [(i, i ^ 1) for i in range(32)])  4.29 us
    pallas_call x1, Pallas kernels, compact(): pl.pallas_call(functools.partial(compact_kernel, first, slots), in_specs=...  2.4 us
  transfers between devices with their start and end apart: 14, of which 2 were waited for; matrix products, arithmetic and copies ran while one was open for 5% of the time, Pallas kernels for 37%

commit v1 on v0

--- a/solution.py
+++ b/solution.py
@@ -66,7 +66,7 @@
                         }
                         for piece in ((1, 2), (3, 4), (5, 6), (7,))[chunk]:
                             spot = one[piece][side]
-                            groups += [place(*spot, 0), place(*spot, 1)]
+                            groups += [place(*spot, side), place(*spot, 1 - side)]
                         if chunk == 3:
                             groups += [place(y, z, side), place(y + 2, z ^ 3, side)]
                 table[place(y, z, core)] = groups
@@ -87,22 +87,38 @@
 LABELS = 16
 
 
-def join_kernel(core_ref, own, other, after, out):
-    core = core_ref[0]
-    out[pl.ds(pl.multiple_of(core * 32, 32), 32), :] = own[...]
-    out[pl.ds(pl.multiple_of(32 - core * 32, 32), 32), :] = other[...]
-
-
-def join_cores(core, own, other, after):
+def join_kernel(own, other, after, out):
+    rows = own.shape[0]
+    out[:rows, :] = own[...]
+    out[rows:, :] = other[...]
+
+
+def join_cores(own, other, after):
     rows, columns = own.shape
     return pl.pallas_call(
         join_kernel,
-        in_specs=[SMEM, VMEM, VMEM, ANY],
+        in_specs=[VMEM, VMEM, ANY],
         out_specs=VMEM,
         out_shape=jax.ShapeDtypeStruct((2 * rows, columns), BF),
         compiler_params=params(8),
         cost_estimate=cost(0, 4 * rows * columns * 2),
-    )(core, own, other, after)
+    )(own, other, after)
+
+
+def gate_kernel(*refs):
+    pass
+
+
+def gate(array, *after):
+    return pl.pallas_call(
+        gate_kernel,
+        in_specs=[ANY] * (1 + len(after)),
+        out_specs=ANY,
+        out_shape=jax.ShapeDtypeStruct(array.shape, array.dtype),
+        input_output_aliases={0: 0},
+        compiler_params=params(1),
+        cost_estimate=cost(0, 0),
+    )(array, *after)
 
 
 def ranks_of(labels, blocks):
@@ -245,29 +261,58 @@
 
 
 def turn_kernel(edge, count, *refs):
-    pieces, out, held = refs[:count], refs[-2], refs[-1]
-    for i in range(edge * edge // WIDE):
-        columns = slice(i * WIDE, (i + 1) * WIDE)
-        turned = jnp.concatenate([piece[:, columns] for piece in pieces], 0).T
-        out[columns, :WIDE] = turned
-        held[columns, :] = turned.astype(F32)
+    pieces = refs[:count]
+    out, rows, held, both, arrived, left = refs[-6:]
+    columns = edge * edge
+    parts = 4
+    wide = columns // parts
+    starts = [sum(piece.shape[0] for piece in pieces[:i]) for i in range(count)]
+
+    def arrival(i, part):
+        at = pl.ds(part * wide, wide)
+        there = rows.at[pl.ds(starts[i], pieces[i].shape[0]), at]
+        return pltpu.make_async_copy(pieces[i].at[:, at], there, arrived.at[i, part])
+
+    for part in range(parts):
+        for i in range(count):
+            arrival(i, part).start()
+    for part in range(parts):
+        for i in range(count):
+            arrival(i, part).wait()
+        for i in range(part * wide // WIDE, (part + 1) * wide // WIDE):
+            at = slice(i * WIDE, (i + 1) * WIDE)
+            turned = rows[:, at].T
+            both[at, :WIDE] = turned
+            held[at, :] = turned.astype(F32)
+    copies = []
     for low in range(0, edge, 8):
-        parts = []
+        groups = []
         for b in range(0, edge, 8):
-            rows = [held[(b + i) * edge + low : (b + i) * edge + low + 8, :] for i in range(8)]
-            parts.append(jnp.swapaxes(jnp.stack(rows, 0), 0, 1))
-        whole = jnp.concatenate(parts, 1)
-        out[low * edge : (low + 8) * edge, WIDE:] = whole.reshape(8 * edge, WIDE).astype(BF)
+            group = [held[(b + i) * edge + low : (b + i) * edge + low + 8, :] for i in range(8)]
+            groups.append(jnp.swapaxes(jnp.stack(group, 0), 0, 1))
+        whole = jnp.concatenate(groups, 1)
+        at = pl.ds(low * edge, 8 * edge)
+        both[low * edge : (low + 8) * edge, WIDE:] = whole.reshape(8 * edge, WIDE).astype(BF)
+        copies.append(pltpu.make_async_copy(both.at[at, :], out.at[at, :], left.at[low // 8]))
+        copies[-1].start()
+    for copy in copies:
+        copy.wait()
 
 
 def turn(edge, pieces, after=()):
     columns = edge * edge
     return pl.pallas_call(
         functools.partial(turn_kernel, edge, len(pieces)),
-        in_specs=[VMEM] * len(pieces) + [ANY] * len(after),
-        out_specs=VMEM,
+        in_specs=[ANY] * (len(pieces) + len(after)),
+        out_specs=ANY,
         out_shape=jax.ShapeDtypeStruct((columns, 2 * WIDE), BF),
-        scratch_shapes=[pltpu.VMEM((columns, WIDE), F32)],
+        scratch_shapes=[
+            pltpu.VMEM((WIDE, columns), BF),
+            pltpu.VMEM((columns, WIDE), F32),
+            pltpu.VMEM((columns, 2 * WIDE), BF),
+            pltpu.SemaphoreType.DMA((len(pieces), 4)),
+            pltpu.SemaphoreType.DMA((edge // 8,)),
+        ],
         compiler_params=params(12),
         cost_estimate=cost(columns * WIDE * 2, columns * WIDE * 6),
     )(*pieces, *after)
@@ -333,7 +378,6 @@
     edge = virt_energy.shape[1]
     columns = edge * edge
     me = lax.axis_index("pair")
-    core = (me % 2).astype(I32)
     own = integrals.reshape(integrals.shape[0], columns)
 
     packed = compact(0, SLOTS, cd_irrep, pair_irrep, amplitudes)
@@ -348,19 +392,18 @@
 
     spill = lax.cond(same.max() > SLOTS, more, none)
 
-    block = join_cores(core.reshape(1), own, swap_cores(own), packed)
+    block = join_cores(own, swap_cores(own), packed)
     p1 = send(block, along_y(1), along_y(-1))
     p2 = send(block, along_z(1), along_z(2))
     p3 = send(block, along_z(3), along_y(2))
+    order = jnp.asarray(order_table())[me]
+    p2 = gate(p2, spill, order)
     p4 = send(p2, along_y(1), along_y(1))
     p5 = send(p2, along_y(-1), along_y(-1))
+    left = left_sides(cd_irrep, pair_irrep, mirror_tile, order, amplitudes, sent, spill)
     p6 = send(p3, along_y(1), along_z(1))
     p7 = send(p3, along_y(-1), along_z(2))
-    half = lax.dynamic_slice(p3, (core * 32, jnp.int32(0)), (32, columns))
-    p8 = send(half, along_y(2), along_z(3))
-
-    order = jnp.asarray(order_table())[me]
-    left = left_sides(cd_irrep, pair_irrep, mirror_tile, order, amplitudes, sent, spill)
+    p8 = send(p3[: own.shape[0]], along_y(2), along_z(3))
 
     sides = []
     for pieces, after in (((p1, p2), (sent, spill)), ((p3, p4), (left,)), ((p5, p6), ()), ((p7, own, p8), ())):

time: 86 us -> 83.1 us (0.966)
  Pallas kernels: 44.8 us -> 42.2 us
    pallas_call x4, Pallas kernels: 12.8 us -> 10.7 us  [turn(): pl.pallas_call(functools.partial(turn_kernel, edge, len(pieces)), in_spec...]
    dynamic_slice x1 -> x0, local copies, waits for them, and re-layouts: 1.7 us -> none  [body(): half = lax.dynamic_slice(p3, (core * 32, jnp.int32(0)), (32, columns))]
    slice x0 -> x1, local copies, waits for them, and re-layouts: none -> 1 us  [body(): p8 = send(p3[:own.shape[0]], along_y(2), along_z(3))]
  transfers between devices with their start and end apart: 14 -> 14, of which waited for: 2 -> 2; matrix products, arithmetic and copies ran while one was open for 5% -> 4% of each run, Pallas kernels for 37% -> 35%
where the time goes in v1:
time: 83.1 us; the launch traced here: 82.8 us
  Pallas kernels  42.2 us (51%)
  waiting for transfers between devices  18 us (22%)
  starting transfers between devices  17.3 us (21%)
  local copies, waits for them, and re-layouts  3.62 us (4%)
  other arithmetic  0.89 us (1%)
  between operations  0.89 us (1%)
    pallas_call x2, Pallas kernels, ladder(): pl.pallas_call(functools.partial(ladder_kernel, len(sides), last), grid=(...  24.7 us
    ppermute x9, waiting for transfers between devices, send(): return lax.ppermute(array, 'pair', pairs_of(first, second))  17.9 us
    ppermute x9, starting transfers between devices, send(): return lax.ppermute(array, 'pair', pairs_of(first, second))  12.7 us
    pallas_call x4, Pallas kernels, turn(): pl.pallas_call(functools.partial(turn_kernel, edge, len(pieces)), in_spec...  10.7 us
    ppermute x5, starting transfers between devices, swap_cores(): return lax.ppermute(array, 'pair', [(i, i ^ 1) for i in range(32)])  4.59 us
    pallas_call x1, Pallas kernels, left_sides(): pl.pallas_call(left_kernel, in_specs=[SMEM] * 4 + [VMEM] * 3, out_specs=V...  4.37 us
    pallas_call x1, Pallas kernels, compact(): pl.pallas_call(functools.partial(compact_kernel, first, slots), in_specs=...  2.4 us
  transfers between devices with their start and end apart: 14, of which 2 were waited for; matrix products, arithmetic and copies ran while one was open for 4% of the time, Pallas kernels for 35%

profile of v1, /device:TPU:1, one launch (start us, length us, event | category | flops | bytes accessed | tf_op | source)
XLA Modules:
  0.0 82.8 jit_solution(3128865328311393752)
XLA Ops:
  0.0 3.2 %collective-permute-start.2 = (bf16[32,4096]{1,0:T(8,128)(2,1)}, bf16[32,4096]{1,0:T(8,128)(2,1)S(1)}, u32[]{:S(2)}, u32[]{:S(2)}) collective-permute-start(bf16[32,4096]{1,0:T(8,128)(2,1)} %bitcast.5), channel_id=1, source_target_pairs={{0,8},{8,0},{16,24},{24,16},{32,40},{40,32},{48,56},{56,48},{64,72... | collective-permute-start | bytes 786440 | tf_op jit(solution)/shard_map/ppermute | solution.py:47
  3.2 2.4 %shard_map.82.after = bf16[784,256]{1,0:T(8,128)(2,1)S(1)} custom-call(s32[16]{0:T(128)} %cd.3, s32[12]{0:T(128)} %irreps.3, bf16[768,1024]{1,0:T(8,128)(2,1)} %amplitudes.3), custom_call_target="tpu_custom_call" | custom-call | tf_op jit(solution)/shard_map/pallas_call | solution.py:169
  5.7 0.0 collective-permute-done.2.other
  5.7 1.4 %collective-permute-start.3 = (bf16[64,4096]{1,0:T(8,128)(2,1)S(1)}, bf16[64,4096]{1,0:T(8,128)(2,1)}, u32[]{:S(2)}, u32[]{:S(2)}) collective-permute-start(bf16[64,4096]{1,0:T(8,128)(2,1)S(1)} %shard_map.84), channel_id=1, source_target_pairs={{0,16},{8,40},{16,0},{24,56},{32,48},{40,8},{48,32},{56,24},{64,80... | collective-permute-start | bytes 1572872 | tf_op jit(solution)/shard_map/ppermute | solution.py:43
  7.1 2.9 %collective-permute-start.5 = (bf16[64,4096]{1,0:T(8,128)(2,1)S(1)}, bf16[64,4096]{1,0:T(8,128)(2,1)}, u32[]{:S(2)}, u32[]{:S(2)}) collective-permute-start(bf16[64,4096]{1,0:T(8,128)(2,1)S(1)} %shard_map.84), channel_id=1, source_target_pairs={{0,48},{8,136},{16,32},{24,152},{32,16},{40,168},{48,0},{56,184},{... | collective-permute-start | bytes 1572872 | tf_op jit(solution)/shard_map/ppermute | solution.py:43
  10.1 0.1 collective-permute-start.1
  10.1 2.7 %collective-permute-start.11 = (bf16[64,4096]{1,0:T(8,128)(2,1)S(1)}, bf16[64,4096]{1,0:T(8,128)(2,1)S(1)}, u32[]{:S(2)}, u32[]{:S(2)}) collective-permute-start(bf16[64,4096]{1,0:T(8,128)(2,1)S(1)} %shard_map.84), channel_id=1, source_target_pairs={{0,64},{8,200},{16,80},{24,216},{32,96},{40,232},{48,112},{56,248}... | collective-permute-start | bytes 1572872 | tf_op jit(solution)/shard_map/ppermute | solution.py:43
  12.9 0.2 convert_reduce_fusion
  13.0 0.6 reduce_max.9
  14.3 0.0 copy-start.4
  14.4 0.9 %conditional.1 = (bf16[784,384]{1,0:T(8,128)(2,1)}) conditional(s32[]{:T(128)} %convert_element_type.7, () %tuple.11, (s32[16]{0:T(128)S(1)}, s32[12]{0:T(128)S(1)}, bf16[768,1024]{1,0:T(8,128)(2,1)}) %tuple.16), branch_computations={%region_2.0_spmd, %region_3.0_spmd} | conditional | bytes 2408496 | solution.py:393
  14.4 0.9 %broadcast.8 = bf16[784,384]{1,0:T(8,128)(2,1)} broadcast(bf16[]{:T(256)} %constant.3.clone), dimensions={} | broadcast | bytes 602114 | tf_op jit(solution)/shard_map/broadcast.1
  15.2 0.8 dynamic-slice_bitcast_fusion.order.refs_2_
  16.1 15.2 %collective-permute-done.3.refs_0_ = bf16[64,4096]{1,0:T(8,128)(2,1)} collective-permute-done((bf16[64,4096]{1,0:T(8,128)(2,1)S(1)}, bf16[64,4096]{1,0:T(8,128)(2,1)}, u32[]{:S(2)}, u32[]{:S(2)}) %collective-permute-start.3) | collective-permute-done | bytes 524320 | tf_op jit(solution)/shard_map/ppermute | solution.py:43
  31.3 0.0 collective-permute-start.13
  31.3 2.7 %collective-permute-start.4 = (bf16[64,4096]{1,0:T(8,128)(2,1)}, bf16[64,4096]{1,0:T(8,128)(2,1)S(1)}, u32[]{:S(2)}, u32[]{:S(2)}) collective-permute-start(bf16[64,4096]{1,0:T(8,128)(2,1)} %shard_map.85.refs_1_), channel_id=1, source_target_pairs={{0,192},{8,200},{16,208},{24,216},{32,224},{40,232},{48,240},{56,2... | collective-permute-start | bytes 1572872 | tf_op jit(solution)/shard_map/ppermute | solution.py:43
  34.0 0.0 collective-permute-done.5.refs_0_
  34.0 0.0 collective-permute-start.6
  34.0 0.0 collective-permute-done.1.sent.refs_2_
  34.0 2.9 %collective-permute-start.8 = (bf16[64,4096]{1,0:T(8,128)(2,1)}, bf16[64,4096]{1,0:T(8,128)(2,1)S(1)}, u32[]{:S(2)}, u32[]{:S(2)}) collective-permute-start(bf16[64,4096]{1,0:T(8,128)(2,1)} %collective-permute-done.5.refs_0_), channel_id=1, source_target_pairs={{0,192},{8,40},{16,208},{24,56},{32,224},{40,8},{48,240},{56,24},{... | collective-permute-start | bytes 1572872 | tf_op jit(solution)/shard_map/ppermute | solution.py:43
  36.8 1.0 %slice.4 = bf16[32,4096]{1,0:T(8,128)(2,1)S(1)} slice(bf16[64,4096]{1,0:T(8,128)(2,1)} %collective-permute-done.5.refs_0_), slice={[0:32], [0:4096]} | slice | bytes 524288 | tf_op jit(solution)/shard_map/slice | solution.py:406
  37.9 2.7 %collective-permute-done.11.refs_0_ = bf16[64,4096]{1,0:T(8,128)(2,1)S(1)} collective-permute-done((bf16[64,4096]{1,0:T(8,128)(2,1)S(1)}, bf16[64,4096]{1,0:T(8,128)(2,1)S(1)}, u32[]{:S(2)}, u32[]{:S(2)}) %collective-permute-start.11) | collective-permute-done | bytes 524320 | tf_op jit(solution)/shard_map/ppermute | solution.py:43
  40.5 0.8 copy-done.2
  41.3 0.0 collective-permute-start.9
  41.3 0.0 copy-start.3
  41.3 4.4 %shard_map.83.refs_2_.refs_0_ = bf16[768,2048]{1,0:T(8,128)(2,1)S(1)} custom-call(s32[16]{0:T(128)S(1)} %copy-done.6, s32[12]{0:T(128)} %irreps.3, s32[12]{0:T(128)S(1)} %copy-done.4, s32[32]{0:T(128)S(1)} %dynamic-slice_bitcast_fusion.order.refs_2_, bf16[768,1024]{1,0:T(8,128)(2,1)S(1)} %copy-done.5, ...), custom_call_target="tpu_custom_call" | custom-call | tf_op jit(solution)/shard_map/pallas_call | solution.py:252
  45.7 3.0 %shard_map.88.refs_1_ = bf16[4096,256]{1,0:T(8,128)(2,1)} custom-call(bf16[64,4096]{1,0:T(8,128)(2,1)S(1)} %copy-done.3, bf16[64,4096]{1,0:T(8,128)(2,1)} %shard_map.85.refs_1_, bf16[784,256]{1,0:T(8,128)(2,1)S(1)} %collective-permute-done.1.sent.refs_2_, bf16[784,384]{1,0:T(8,128)(2,1)} %get-tuple-element.17.spill.refs_1_.refs_3_), custom_call_target="tpu_custom_call" | custom-call | tf_op jit(solution)/shard_map/pallas_call | solution.py:304
  48.7 0.0 collective-permute-done.13.refs_1_
  48.8 0.1 collective-permute-start.12
  48.9 3.0 %shard_map.89.refs_3_ = bf16[4096,256]{1,0:T(8,128)(2,1)} custom-call(bf16[64,4096]{1,0:T(8,128)(2,1)} %collective-permute-done.5.refs_0_, bf16[64,4096]{1,0:T(8,128)(2,1)S(1)} %collective-permute-done.13.refs_1_, bf16[768,2048]{1,0:T(8,128)(2,1)S(1)} %shard_map.83.refs_2_.refs_0_), custom_call_target="tpu_custom_call" | custom-call | tf_op jit(solution)/shard_map/pallas_call | solution.py:304
  51.9 0.0 copy-start.1
  51.9 0.0 collective-permute-done.4.refs_0_
  51.9 0.6 collective-permute-start.14
  52.5 0.0 collective-permute-done.6.refs_1_
  52.5 2.3 %shard_map.86.refs_1_ = bf16[4096,256]{1,0:T(8,128)(2,1)} custom-call(bf16[64,4096]{1,0:T(8,128)(2,1)S(1)} %collective-permute-done.4.refs_0_, bf16[64,4096]{1,0:T(8,128)(2,1)S(1)} %collective-permute-done.6.refs_1_), custom_call_target="tpu_custom_call" | custom-call | tf_op jit(solution)/shard_map/pallas_call | solution.py:304
  54.7 0.0 copy-start.9
  54.8 0.0 copy-start.8
  54.8 0.1 collective-permute-start.7
  54.9 2.4 %shard_map.87.refs_3_ = bf16[4096,256]{1,0:T(8,128)(2,1)} custom-call(bf16[64,4096]{1,0:T(8,128)(2,1)S(1)} %collective-permute-done.8.refs_0_, bf16[32,4096]{1,0:T(8,128)(2,1)S(1)} %bitcast.7, bf16[32,4096]{1,0:T(8,128)(2,1)S(1)} %collective-permute-done.9.refs_2_), custom_call_target="tpu_custom_call" | custom-call | tf_op jit(solution)/shard_map/pallas_call | solution.py:304
  57.3 0.6 collective-permute-start.10
  57.9 0.1 broadcast_add_fusion
  58.0 0.1 add.33.refs_7_
  58.1 0.0 collective-permute-done.12.refs_2_
  58.1 0.0 collective-permute-done.14.refs_4_
  58.1 11.5 %shard_map.90.refs_5_ = f32[768,4096]{1,0:T(8,128)} custom-call(bf16[768,2048]{1,0:T(8,128)(2,1)S(1)} %shard_map.83.refs_2_.refs_0_, bf16[4096,256]{1,0:T(8,128)(2,1)} %shard_map.88.refs_1_, bf16[4096,256]{1,0:T(8,128)(2,1)} %collective-permute-done.12.refs_2_, bf16[4096,256]{1,0:T(8,128)(2,1)} %shard_map.89.refs_3_, ...), custom_call_target="tpu_custom_call" | custom-call | tf_op jit(solution)/shard_map/pallas_call | solution.py:364
  69.6 0.0 collective-permute-done.7.refs_2_
  69.6 0.0 collective-permute-done.10.refs_4_
  69.6 13.2 %shard_map.91 = bf16[768,4096]{1,0:T(8,128)(2,1)} custom-call(bf16[768,2048]{1,0:T(8,128)(2,1)S(1)} %shard_map.83.refs_2_.refs_0_, bf16[4096,256]{1,0:T(8,128)(2,1)} %shard_map.86.refs_1_, bf16[4096,256]{1,0:T(8,128)(2,1)} %collective-permute-done.7.refs_2_, bf16[4096,256]{1,0:T(8,128)(2,1)} %shard_map.87.refs_3_, ...), custom_call_target="tpu_custom_call" | custom-call | tf_op jit(solution)/shard_map/pallas_call | solution.py:364
  (19 shorter events, 0.1 us)
Async XLA Ops:
  0.0 5.7 %copy-start = (bf16[32,1,4096]{2,0,1:T(8,128)(2,1)S(1)}, bf16[32,1,4096]{2,0,1:T(8,128)(2,1)}, u32[]{:S(2)}) copy-start(bf16[32,1,4096]{2,0,1:T(8,128)(2,1)} %param.11) | copy-start | bytes 786436
  0.0 14.3 %copy-start.7 = (s32[12]{0:T(128)S(1)}, s32[12]{0:T(128)}, u32[]{:S(2)}) copy-start(s32[12]{0:T(128)} %irreps.3) | copy-start | bytes 148
  0.0 12.9 %copy-start.6 = (s32[16]{0:T(128)S(1)}, s32[16]{0:T(128)}, u32[]{:S(2)}) copy-start(s32[16]{0:T(128)} %cd.3) | copy-start | bytes 196
  0.0 5.6 %collective-permute-start.2 = (bf16[32,4096]{1,0:T(8,128)(2,1)}, bf16[32,4096]{1,0:T(8,128)(2,1)S(1)}, u32[]{:S(2)}, u32[]{:S(2)}) collective-permute-start(bf16[32,4096]{1,0:T(8,128)(2,1)} %bitcast.5), channel_id=1, source_target_pairs={{0,8},{8,0},{16,24},{24,16},{32,40},{40,32},{48,56},{56,48},{64,72... | collective-permute-start | bytes 786440 | tf_op jit(solution)/shard_map/ppermute | solution.py:47
  5.7 25.6 %collective-permute-start.3 = (bf16[64,4096]{1,0:T(8,128)(2,1)S(1)}, bf16[64,4096]{1,0:T(8,128)(2,1)}, u32[]{:S(2)}, u32[]{:S(2)}) collective-permute-start(bf16[64,4096]{1,0:T(8,128)(2,1)S(1)} %shard_map.84), channel_id=1, source_target_pairs={{0,16},{8,40},{16,0},{24,56},{32,48},{40,8},{48,32},{56,24},{64,80... | collective-permute-start | bytes 1572872 | tf_op jit(solution)/shard_map/ppermute | solution.py:43
  7.1 26.8 %collective-permute-start.5 = (bf16[64,4096]{1,0:T(8,128)(2,1)S(1)}, bf16[64,4096]{1,0:T(8,128)(2,1)}, u32[]{:S(2)}, u32[]{:S(2)}) collective-permute-start(bf16[64,4096]{1,0:T(8,128)(2,1)S(1)} %shard_map.84), channel_id=1, source_target_pairs={{0,48},{8,136},{16,32},{24,152},{32,16},{40,168},{48,0},{56,184},{... | collective-permute-start | bytes 1572872 | tf_op jit(solution)/shard_map/ppermute | solution.py:43
  10.1 23.9 %collective-permute-start.1 = (bf16[784,256]{1,0:T(8,128)(2,1)S(1)}, bf16[784,256]{1,0:T(8,128)(2,1)S(1)}, u32[]{:S(2)}, u32[]{:S(2)}) collective-permute-start(bf16[784,256]{1,0:T(8,128)(2,1)S(1)} %shard_map.82.after), channel_id=1, source_target_pairs={{0,128},{8,136},{16,144},{24,152},{32,160},{40,168},{48,176},{56,1... | collective-permute-start | bytes 1204232 | tf_op jit(solution)/shard_map/ppermute | solution.py:43
  10.1 30.4 %collective-permute-start.11 = (bf16[64,4096]{1,0:T(8,128)(2,1)S(1)}, bf16[64,4096]{1,0:T(8,128)(2,1)S(1)}, u32[]{:S(2)}, u32[]{:S(2)}) collective-permute-start(bf16[64,4096]{1,0:T(8,128)(2,1)S(1)} %shard_map.84), channel_id=1, source_target_pairs={{0,64},{8,200},{16,80},{24,216},{32,96},{40,232},{48,112},{56,248}... | collective-permute-start | bytes 1572872 | tf_op jit(solution)/shard_map/ppermute | solution.py:43
  14.3 27.0 %copy-start.4 = (s32[12]{0:T(128)S(1)}, s32[12]{0:T(128)}, u32[]{:S(2)}) copy-start(s32[12]{0:T(128)} %mirror.1) | copy-start | bytes 148
  15.2 26.1 %copy-start.5 = (bf16[768,1024]{1,0:T(8,128)(2,1)S(1)}, bf16[768,1024]{1,0:T(8,128)(2,1)}, u32[]{:S(2)}) copy-start(bf16[768,1024]{1,0:T(8,128)(2,1)} %amplitudes.3) | copy-start | bytes 4718596
  31.3 17.4 %collective-permute-start.13 = (bf16[64,4096]{1,0:T(8,128)(2,1)}, bf16[64,4096]{1,0:T(8,128)(2,1)S(1)}, u32[]{:S(2)}, u32[]{:S(2)}) collective-permute-start(bf16[64,4096]{1,0:T(8,128)(2,1)} %shard_map.85.refs_1_), channel_id=1, source_target_pairs={{0,64},{8,72},{16,80},{24,88},{32,96},{40,104},{48,112},{56,120},{... | collective-permute-start | bytes 1572872 | tf_op jit(solution)/shard_map/ppermute | solution.py:43
  31.3 20.6 %collective-permute-start.4 = (bf16[64,4096]{1,0:T(8,128)(2,1)}, bf16[64,4096]{1,0:T(8,128)(2,1)S(1)}, u32[]{:S(2)}, u32[]{:S(2)}) collective-permute-start(bf16[64,4096]{1,0:T(8,128)(2,1)} %shard_map.85.refs_1_), channel_id=1, source_target_pairs={{0,192},{8,200},{16,208},{24,216},{32,224},{40,232},{48,240},{56,2... | collective-permute-start | bytes 1572872 | tf_op jit(solution)/shard_map/ppermute | solution.py:43
  34.0 18.5 %collective-permute-start.6 = (bf16[64,4096]{1,0:T(8,128)(2,1)}, bf16[64,4096]{1,0:T(8,128)(2,1)S(1)}, u32[]{:S(2)}, u32[]{:S(2)}) collective-permute-start(bf16[64,4096]{1,0:T(8,128)(2,1)} %collective-permute-done.5.refs_0_), channel_id=1, source_target_pairs={{0,64},{8,24},{16,80},{24,8},{32,96},{40,56},{48,112},{56,40},{64,... | collective-permute-start | bytes 1572872 | tf_op jit(solution)/shard_map/ppermute | solution.py:43
  34.0 20.9 %collective-permute-start.8 = (bf16[64,4096]{1,0:T(8,128)(2,1)}, bf16[64,4096]{1,0:T(8,128)(2,1)S(1)}, u32[]{:S(2)}, u32[]{:S(2)}) collective-permute-start(bf16[64,4096]{1,0:T(8,128)(2,1)} %collective-permute-done.5.refs_0_), channel_id=1, source_target_pairs={{0,192},{8,40},{16,208},{24,56},{32,224},{40,8},{48,240},{56,24},{... | collective-permute-start | bytes 1572872 | tf_op jit(solution)/shard_map/ppermute | solution.py:43
  40.5 0.8 copy-start.2
  41.3 13.6 %collective-permute-start.9 = (bf16[32,4096]{1,0:T(8,128)(2,1)S(1)}, bf16[32,4096]{1,0:T(8,128)(2,1)S(1)}, u32[]{:S(2)}, u32[]{:S(2)}) collective-permute-start(bf16[32,4096]{1,0:T(8,128)(2,1)S(1)} %slice.4), channel_id=1, source_target_pairs={{0,128},{8,56},{16,144},{24,40},{32,160},{40,24},{48,176},{56,8},{... | collective-permute-start | bytes 786440 | tf_op jit(solution)/shard_map/ppermute | solution.py:43
  41.3 4.4 %copy-start.3 = (bf16[64,4096]{1,0:T(8,128)(2,1)S(1)}, bf16[64,4096]{1,0:T(8,128)(2,1)}, u32[]{:S(2)}) copy-start(bf16[64,4096]{1,0:T(8,128)(2,1)} %copy-done.2) | copy-start | bytes 1572868
  48.8 9.3 %collective-permute-start.12 = (bf16[4096,256]{1,0:T(8,128)(2,1)}, bf16[4096,256]{1,0:T(8,128)(2,1)}, u32[]{:S(2)}, u32[]{:S(2)}) collective-permute-start(bf16[4096,256]{1,0:T(8,128)(2,1)} %shard_map.88.refs_1_), channel_id=1, source_target_pairs={{0,8},{8,0},{16,24},{24,16},{32,40},{40,32},{48,56},{56,48},{64,72... | collective-permute-start | bytes 6291464 | tf_op jit(solution)/shard_map/ppermute | solution.py:47
  51.9 3.0 %copy-start.1 = (bf16[32,1,4096]{2,0,1:T(8,128)(2,1)S(1)}, bf16[32,1,4096]{2,0,1:T(8,128)(2,1)}, u32[]{:S(2)}) copy-start(bf16[32,1,4096]{2,0,1:T(8,128)(2,1)} %param.11) | copy-start | bytes 786436
  51.9 6.2 %collective-permute-start.14 = (bf16[4096,256]{1,0:T(8,128)(2,1)}, bf16[4096,256]{1,0:T(8,128)(2,1)}, u32[]{:S(2)}, u32[]{:S(2)}) collective-permute-start(bf16[4096,256]{1,0:T(8,128)(2,1)} %shard_map.89.refs_3_), channel_id=1, source_target_pairs={{0,8},{8,0},{16,24},{24,16},{32,40},{40,32},{48,56},{56,48},{64,72... | collective-permute-start | bytes 6291464 | tf_op jit(solution)/shard_map/ppermute | solution.py:47
  54.7 3.2 %copy-start.9 = (f32[1,64]{1,0:T(1,128)S(1)}, f32[1,64]{1,0:T(1,128)}, u32[]{:S(2)}) copy-start(f32[1,64]{1,0:T(1,128)} %param.16) | copy-start | bytes 772
  54.8 3.3 %copy-start.8 = (f32[768]{0:T(1024)S(1)}, f32[768]{0:T(1024)}, u32[]{:S(2)}) copy-start(f32[768]{0:T(1024)} %param.15) | copy-start | bytes 9220
  54.8 14.8 %collective-permute-start.7 = (bf16[4096,256]{1,0:T(8,128)(2,1)}, bf16[4096,256]{1,0:T(8,128)(2,1)}, u32[]{:S(2)}, u32[]{:S(2)}) collective-permute-start(bf16[4096,256]{1,0:T(8,128)(2,1)} %shard_map.86.refs_1_), channel_id=1, source_target_pairs={{0,8},{8,0},{16,24},{24,16},{32,40},{40,32},{48,56},{56,48},{64,72... | collective-permute-start | bytes 6291464 | tf_op jit(solution)/shard_map/ppermute | solution.py:47
  57.3 12.3 %collective-permute-start.10 = (bf16[4096,256]{1,0:T(8,128)(2,1)}, bf16[4096,256]{1,0:T(8,128)(2,1)}, u32[]{:S(2)}, u32[]{:S(2)}) collective-permute-start(bf16[4096,256]{1,0:T(8,128)(2,1)} %shard_map.87.refs_3_), channel_id=1, source_target_pairs={{0,8},{8,0},{16,24},{24,16},{32,40},{40,32},{48,56},{56,48},{64,72... | collective-permute-start | bytes 6291464 | tf_op jit(solution)/shard_map/ppermute | solution.py:47
